TPU v7x, 32 devices: a whole 2x2x4 slice. The times are simulated.
32 devices in a mesh: groups: 2 (over y), space: 4 (over z), tangent: 4 (over x, core).
Axes of the slice: x: 2, y: 2, z: 4, core: 2. Of those that a mesh axis runs over, the one named last changes fastest.
Arguments:
- positions: float32 [16, 2, 128], P(('groups', 'space')), parts along dimension 0, may hold values from 0.45 to 15.55, as said below
- momenta: float32 [16, 2, 128], P(('groups', 'space')), parts along dimension 0, may hold values from -4 to 4
- cell_count: int32 [16], P(('groups', 'space')), parts along dimension 0, may hold values from 64 to 128, as said below
- tangent: float32 [16, 4, 128, 1024], P(('groups', 'space'), None, None, 'tangent'), parts along dimension 0, may hold values from -6 to 6
Outputs:
- phase: float32 [16, 4, 128], P(('groups', 'space')), parts along dimension 0
- new_tangent: float32 [16, 4, 128, 1024], P(('groups', 'space'), None, None, 'tangent'), parts along dimension 0
- stretch: float32 [2048], P(('groups', 'tangent')), parts along dimension 0
There are 2 independent parts, one for each index of `groups`. A program takes and returns all parts, laid end to end along the dimension named above; each array names one. Nothing has to cross between parts.
Inputs may be any that keep to these rules, and one draw needn't show every extreme that they name: Slots 0 to cell_count - 1 of a cell hold particles, the others are padding; some cell holds 128 particles in every draw. `positions`: every slot of a cell, padding too, lies within 0.05 in each coordinate of its own point of the lattice (m + 0.5, n + 0.5), m from 0 to 7, n from 0 to 15; no two slots of a cell share a lattice point.
All inputs are finite; a program needn't handle non-finite values.
Results may differ from a plain program's by a relative error of at most 0.006.
Values may be sent and summed in bfloat16 or wider, within the bound.
No kernel may reach another device: no remote copies, remote signals or barrier semaphores. Data moves between devices by JAX's collectives and lax.ppermute only.
A program may use at most 128 MiB of HBM per device.

v0:
```python
import jax
import jax.numpy as jnp
from jax import lax
from jax.sharding import PartitionSpec as P

STEPS = 2
DT = 0.005
CUT2 = 2.0 ** (1.0 / 3.0)
PARK = 1000.0
HIGH = lax.Precision.HIGHEST


def padded(block, sides, width):
    for axis, dim in sides:
        count = lax.axis_size(axis)
        forward = [(i, i + 1) for i in range(count - 1)]
        forward.append((count - 1, 0))
        backward = [(target, source) for source, target in forward]
        low = lax.ppermute(
            lax.slice_in_dim(block, block.shape[dim] - width, None, axis=dim), axis, forward
        )
        high = lax.ppermute(lax.slice_in_dim(block, 0, width, axis=dim), axis, backward)
        block = jnp.concatenate([low, block, high], axis=dim)
    return block


def pair_terms(own_coords, own_alive, far_coords, shift_x, shift_y, same_cell):
    delta_x = shift_x + far_coords[:, 0, None, :] - own_coords[:, 0, :, None]
    delta_y = shift_y + far_coords[:, 1, None, :] - own_coords[:, 1, :, None]
    dist2 = delta_x * delta_x + delta_y * delta_y
    within = jnp.logical_and(dist2 < CUT2, own_alive[:, :, None] > 0.5)
    if same_cell:
        within = jnp.logical_and(within, jnp.logical_not(jnp.eye(dist2.shape[-1], dtype=bool)))
    weight = within.astype(jnp.float32)
    safe = jnp.where(within, dist2, CUT2)
    inverse = 1.0 / safe
    inv_three = inverse * inverse * inverse
    inv_six = inv_three * inv_three
    energy = 4.0 * (inv_six - inv_three) + 1.0
    energy_1 = 4.0 * (3.0 * inv_three - 6.0 * inv_six) * inverse
    energy_2 = 4.0 * (42.0 * inv_six - 12.0 * inv_three) * inverse * inverse
    taper = 1.0 - safe / CUT2
    switch = taper * taper
    switch_1 = -2.0 * taper / CUT2
    switch_2 = 2.0 / (CUT2 * CUT2)
    grad_1 = (energy_1 * switch + energy * switch_1) * weight
    grad_2 = (energy_2 * switch + 2.0 * energy_1 * switch_1 + energy * switch_2) * weight
    pull_x = 2.0 * grad_1 * delta_x
    pull_y = 2.0 * grad_1 * delta_y
    k_xx = (2.0 * grad_1 + 4.0 * grad_2 * delta_x * delta_x).astype(jnp.bfloat16)
    k_xy = (4.0 * grad_2 * delta_x * delta_y).astype(jnp.bfloat16)
    k_yy = (2.0 * grad_1 + 4.0 * grad_2 * delta_y * delta_y).astype(jnp.bfloat16)
    return (pull_x, pull_y, k_xx, k_xy, k_yy)


def apply_rows(k_xx, k_xy, k_yy, far_low):
    gain_x = jnp.einsum(
        "cij,cjv->civ", k_xx, far_low[:, 0], preferred_element_type=jnp.float32
    ) + jnp.einsum("cij,cjv->civ", k_xy, far_low[:, 1], preferred_element_type=jnp.float32)
    gain_y = jnp.einsum(
        "cij,cjv->civ", k_xy, far_low[:, 0], preferred_element_type=jnp.float32
    ) + jnp.einsum("cij,cjv->civ", k_yy, far_low[:, 1], preferred_element_type=jnp.float32)
    return (gain_x, gain_y)


def add_pair(totals, parked, occupied, far_coords, far_low, shift_x, shift_y, same_cell):
    forces_x, forces_y, push_x, push_y, diag_xx, diag_xy, diag_yy = totals
    pull_x, pull_y, k_xx, k_xy, k_yy = pair_terms(
        parked, occupied, far_coords, shift_x, shift_y, same_cell
    )
    gain_x, gain_y = apply_rows(k_xx, k_xy, k_yy, far_low)
    totals = (
        forces_x + jnp.sum(pull_x, axis=2),
        forces_y + jnp.sum(pull_y, axis=2),
        push_x + gain_x,
        push_y + gain_y,
        diag_xx + jnp.sum(k_xx.astype(jnp.float32), axis=2),
        diag_xy + jnp.sum(k_xy.astype(jnp.float32), axis=2),
        diag_yy + jnp.sum(k_yy.astype(jnp.float32), axis=2),
    )
    return (totals, (pull_x, pull_y, k_xx, k_xy, k_yy))


def evaluate(coords, occupied, small_q):
    cell_total = coords.shape[0]
    low = small_q.astype(jnp.bfloat16)
    parked = jnp.concatenate(
        [coords[:, 0:1] + PARK * (1.0 - occupied)[:, None, :], coords[:, 1:2]], axis=1
    )
    empty_rows = jnp.zeros(occupied.shape, jnp.float32)
    empty_push = jnp.zeros(small_q[:, 0].shape, jnp.float32)
    totals = (empty_rows, empty_rows, empty_push, empty_push, empty_rows, empty_rows, empty_rows)
    far_low = padded(low, (("space", 0),), cell_total)
    far_coords = padded(parked, (("space", 0),), cell_total)
    for side in (-1, 0, 1):
        if side == 0:
            block_low = low
            block_coords = parked
        else:
            begin = (1 + side) * cell_total
            block_low = far_low[begin : begin + cell_total]
            block_coords = far_coords[begin : begin + cell_total]
        for lane in (-1, 0, 1):
            totals, unused = add_pair(
                totals,
                parked,
                occupied,
                jnp.roll(block_coords, -lane, axis=0),
                jnp.roll(block_low, -lane, axis=0),
                8.0 * side,
                16.0 * lane,
                side == 0 and lane == 0,
            )
    forces_x, forces_y, push_x, push_y, diag_xx, diag_xy, diag_yy = totals
    wide_own = low.astype(jnp.float32)
    push_x = push_x - diag_xx[..., None] * wide_own[:, 0] - diag_xy[..., None] * wide_own[:, 1]
    push_y = push_y - diag_xy[..., None] * wide_own[:, 0] - diag_yy[..., None] * wide_own[:, 1]
    forces = jnp.stack([forces_x, forces_y], axis=1)
    pushes = jnp.stack([push_x, push_y], axis=1)
    return (forces, pushes)


def body(positions, momenta, cell_count, tangent):
    cell_total = positions.shape[0]
    slot_count = positions.shape[2]
    block_cols = tangent.shape[3]
    occupied = (
        lax.broadcasted_iota(jnp.int32, (cell_total, slot_count), 1) < cell_count[:, None]
    ).astype(jnp.float32)
    state = tangent * occupied[:, None, :, None]
    coords = positions
    speeds = momenta
    small_q = state[:, 0:2]
    small_p = state[:, 2:4]
    forces, pushes = evaluate(coords, occupied, small_q)
    for step_index in range(STEPS):
        midway_p = speeds + 0.5 * DT * forces
        midway_dp = small_p + 0.5 * DT * pushes
        coords = coords + DT * midway_p
        small_q = small_q + DT * midway_dp
        forces, pushes = evaluate(coords, occupied, small_q)
        speeds = midway_p + 0.5 * DT * forces
        small_p = midway_dp + 0.5 * DT * pushes
    phase = jnp.concatenate([coords, speeds], axis=1)
    final = jnp.concatenate([small_q, small_p], axis=1)
    rows_form = lax.all_to_all(final, "tangent", split_axis=2, concat_axis=3, tiled=True)
    full_width = rows_form.shape[3]
    flat_rows = rows_form.reshape(-1, full_width)
    partial_value = lax.dot_general(
        flat_rows,
        flat_rows,
        (((0,), (0,)), ((), ())),
        precision=HIGH,
        preferred_element_type=jnp.float32,
    )
    gram_scale = 1.0 / (4.0 * slot_count * cell_total * lax.axis_size("space"))
    gram = lax.psum(partial_value, ("space", "tangent"))
    factor = jnp.linalg.cholesky(gram * gram_scale)
    solved = jax.scipy.linalg.solve_triangular(factor, flat_rows.T, lower=True).T
    columns_out = lax.all_to_all(
        solved.reshape(rows_form.shape), "tangent", split_axis=3, concat_axis=2, tiled=True
    )
    log_diag = jnp.log(jnp.diagonal(factor))
    stretch = lax.dynamic_slice_in_dim(log_diag, lax.axis_index("tangent") * block_cols, block_cols)
    return (phase, columns_out, stretch)


def solution(mesh):
    placed = (
        P(("groups", "space"), None, None),
        P(("groups", "space"), None, None),
        P(("groups", "space")),
        P(("groups", "space"), None, None, "tangent"),
    )
    return jax.shard_map(
        body,
        mesh=mesh,
        in_specs=placed,
        out_specs=(
            P(("groups", "space"), None, None),
            P(("groups", "space"), None, None, "tangent"),
            P(("groups", "tangent")),
        ),
        check_vma=False,
    )
```

profile of v0, /device:TPU:1, one launch (start us, length us, event | category | flops | bytes accessed | tf_op | source)
XLA Modules:
  0.0 639.7 jit_solution(17771305510368086692)
XLA Ops:
  8.1 4.2 collective-permute-start.1
  14.4 3.3 collective-permute-start.7
  20.4 3.1 convert_reduce_fusion.79
  23.7 3.3 collective-permute-start.3
  27.9 3.4 collective-permute-done.2
  31.3 3.1 convert_reduce_fusion.52
  39.3 3.3 convert_reduce_fusion.25
  59.8 4.8 collective-permute-done.9
  82.1 2.7 collective-permute-done.11
  86.5 7.0 %collective-permute-done.10 = bf16[2,2,128,256]{3,2,0,1:T(8,128)(2,1)S(1)} collective-permute-done((bf16[2,2,128,256]{3,2,0,1:T(8,128)(2,1)S(1)}, bf16[2,2,128,256]{3,2,0,1:T(8,128)(2,1)S(1)}, u32[]{:S(2)}, u32[]{:S(2)}) %collective-permute-start.10) | collective-permute-done | bytes 262176 | tf_op jit(solution)/shard_map/ppermute | solution.py:19
  105.5 21.8 %all_to_all.33 = f32[2,4,128,256]{3,0,1,2:T(2,128)S(1)} all-to-all(f32[2,4,128,256]{3,0,1,2:T(2,128)S(1)} %copy.18), channel_id=1, replica_groups=mesh['groups'=2,'space'=4,'tangent'=4] {'tangent'}, dimensions={2} | all-to-all | bytes 2097152 | tf_op jit(solution)/shard_map/all_to_all | solution.py:146
  128.2 5.2 fusion.2420
  133.8 107.8 %all-reduce.3.cloned.1.call-done = f32[1024,1024]{0,1:T(8,128)} async-done(((f32[1024,1024]{0,1:T(8,128)}), f32[1024,1024]{0,1:T(8,128)}) %all-reduce.3.cloned.1.call-update) | async-done | bytes 4194320 | tf_op jit(solution)/shard_map/psum | solution.py:157
  241.6 5.0 broadcast_multiply_fusion
  246.6 5.7 copy.21
  252.3 4.4 fusion
  258.7 11.7 %cholesky.187 = f32[128,128]{1,0:T(8,128)S(1)} custom-call(f32[128,128]{1,0:T(8,128)S(1)} %cholesky.514), custom_call_target="Cholesky" | custom-call | tf_op jit(solution)/shard_map/jit(cholesky)/cholesky | solution.py:158
  271.1 9.8 %custom-call.63 = f32[1,128,128]{1,2,0:T(8,128)S(1)} custom-call(f32[1,128,128]{2,1,0:T(8,128)S(1)} %get-tuple-element.432), custom_call_target="InvertDiagBlocksLowerTriangular" | custom-call | tf_op jit(solution)/shard_map/jit(cholesky)/cholesky | solution.py:158
  280.9 2.5 cholesky.218
  283.4 2.3 constant_dynamic-update-slice_fusion.32
  287.3 11.9 %cholesky.209 = f32[128,128]{1,0:T(8,128)S(1)} custom-call(f32[128,128]{1,0:T(8,128)S(1)} %cholesky.518), custom_call_target="Cholesky" | custom-call | tf_op jit(solution)/shard_map/jit(cholesky)/cholesky | solution.py:158
  300.5 9.8 %custom-call.64 = f32[1,128,128]{1,2,0:T(8,128)S(1)} custom-call(f32[1,128,128]{2,1,0:T(8,128)S(1)} %get-tuple-element.429), custom_call_target="InvertDiagBlocksLowerTriangular" | custom-call | tf_op jit(solution)/shard_map/jit(cholesky)/cholesky | solution.py:158
  313.6 11.7 %cholesky.402 = f32[128,128]{1,0:T(8,128)S(1)} custom-call(f32[128,128]{1,0:T(8,128)S(1)} %cholesky.523), custom_call_target="Cholesky" | custom-call | tf_op jit(solution)/shard_map/jit(cholesky)/cholesky | solution.py:158
  326.6 9.8 %custom-call.65 = f32[1,128,128]{1,2,0:T(8,128)S(1)} custom-call(f32[1,128,128]{2,1,0:T(8,128)S(1)} %get-tuple-element.426), custom_call_target="InvertDiagBlocksLowerTriangular" | custom-call | tf_op jit(solution)/shard_map/jit(cholesky)/cholesky | solution.py:158
  337.6 2.4 convolution_subtract_fusion.2
  340.0 11.9 %cholesky.421 = f32[128,128]{1,0:T(8,128)S(1)} custom-call(f32[128,128]{1,0:T(8,128)S(1)} %cholesky.528), custom_call_target="Cholesky" | custom-call | tf_op jit(solution)/shard_map/jit(cholesky)/cholesky | solution.py:158
  353.3 9.8 %custom-call.66 = f32[1,128,128]{1,2,0:T(8,128)S(1)} custom-call(f32[1,128,128]{2,1,0:T(8,128)S(1)} %get-tuple-element.423), custom_call_target="InvertDiagBlocksLowerTriangular" | custom-call | tf_op jit(solution)/shard_map/jit(cholesky)/cholesky | solution.py:158
  364.2 2.3 convolution_subtract_fusion.3
  366.5 11.7 %cholesky.440 = f32[128,128]{1,0:T(8,128)S(1)} custom-call(f32[128,128]{1,0:T(8,128)S(1)} %cholesky.533), custom_call_target="Cholesky" | custom-call | tf_op jit(solution)/shard_map/jit(cholesky)/cholesky | solution.py:158
  379.6 10.2 %custom-call.67 = f32[1,128,128]{1,2,0:T(8,128)S(1)} custom-call(f32[1,128,128]{2,1,0:T(8,128)S(1)} %get-tuple-element.420), custom_call_target="InvertDiagBlocksLowerTriangular" | custom-call | tf_op jit(solution)/shard_map/jit(cholesky)/cholesky | solution.py:158
  390.8 2.3 convolution_subtract_fusion.4
  393.1 11.7 %cholesky.460 = f32[128,128]{1,0:T(8,128)S(1)} custom-call(f32[128,128]{1,0:T(8,128)S(1)} %cholesky.538), custom_call_target="Cholesky" | custom-call | tf_op jit(solution)/shard_map/jit(cholesky)/cholesky | solution.py:158
  406.1 9.8 %custom-call.68 = f32[1,128,128]{1,2,0:T(8,128)S(1)} custom-call(f32[1,128,128]{2,1,0:T(8,128)S(1)} %get-tuple-element.417), custom_call_target="InvertDiagBlocksLowerTriangular" | custom-call | tf_op jit(solution)/shard_map/jit(cholesky)/cholesky | solution.py:158
  418.9 11.9 %cholesky.480 = f32[128,128]{1,0:T(8,128)S(1)} custom-call(f32[128,128]{1,0:T(8,128)S(1)} %cholesky.543), custom_call_target="Cholesky" | custom-call | tf_op jit(solution)/shard_map/jit(cholesky)/cholesky | solution.py:158
  432.1 9.8 %custom-call.69 = f32[1,128,128]{1,2,0:T(8,128)S(1)} custom-call(f32[1,128,128]{2,1,0:T(8,128)S(1)} %get-tuple-element.414), custom_call_target="InvertDiagBlocksLowerTriangular" | custom-call | tf_op jit(solution)/shard_map/jit(cholesky)/cholesky | solution.py:158
  444.5 11.7 %cholesky.498 = f32[128,128]{1,0:T(8,128)S(1)} custom-call(f32[128,128]{1,0:T(8,128)S(1)} %convolution_subtract_fusion.13), custom_call_target="Cholesky" | custom-call | tf_op jit(solution)/shard_map/jit(cholesky)/cholesky | solution.py:158
  462.6 6.6 %fusion.1 = (f32[1024,1024]{1,0:T(8,128)}, f32[1024,1024]{1,0:T(8,128)}) fusion(f32[1024,1024]{1,0:T(8,128)} %get-tuple-element.412, pred[]{:T(512)S(6)} %cholesky.513), kind=kLoop, calls=%fused_computation.7 | loop fusion | flops 4194304 | bytes 12582913 | tf_op jit(solution)/shard_map/jit(_solve_triangular)/triangular_solve | solution.py:159
  469.2 23.2 %while.1 = (s32[]{:T(128)}, f32[1024,1024]{1,0:T(8,128)}, s32[8,2]{0,1:T(2,128)S(1)}, f32[8,128,128]{2,1,0:T(8,128)S(1)}, s32[]{:T(128)}) while((s32[]{:T(128)}, f32[1024,1024]{1,0:T(8,128)}, s32[8,2]{0,1:T(2,128)S(1)}, f32[8,128,128]{2,1,0:T(8,128)S(1)}, s32[]{:T(128)}) %tuple.396), condition=%wide.while_cond, body=%wide.while_body.sunk | while | flops 2 | bytes 131189 | solution.py:159
  469.8 2.3 bitcast_dynamic-update-slice_fusion.2
  472.7 2.3 bitcast_dynamic-update-slice_fusion.2
  492.4 79.4 %custom-call.70 = f32[8,128,128]{1,2,0:T(8,128)} custom-call(f32[8,128,128]{2,1,0:T(8,128)S(1)} %get-tuple-element.10), custom_call_target="InvertDiagBlocksLowerTriangular" | custom-call | tf_op jit(solution)/shard_map/jit(_solve_triangular)/triangular_solve | solution.py:159
  587.0 3.1 copy.24
  590.1 5.3 reshape.847
  595.5 5.5 all-to-all-start.1
  601.7 17.3 %gather_fusion = f32[1024]{0:T(1024)S(1)} fusion(f32[1024,1024]{1,0:T(8,128)} %get-tuple-element.320, s32[1024]{0:T(1024)S(1)} %bitcast.397), kind=kCustom, calls=%fused_computation | custom fusion | bytes 16384 | tf_op jit(solution)/shard_map/jit(diagonal)/cond/branch_0_fun/gather | solution.py:163
  620.2 3.7 reduce.48
  623.8 4.2 reshape.848
  628.1 4.6 copy.25
  (302 shorter events, 121.6 us)
Async XLA Ops:
  7.2 234.4 %all-reduce.3.cloned.1.call-start = ((), (), s32[]{:S(2)}) async-start(), calls=%async_computation.2 | async-start | bytes 8388608 | tf_op jit(solution)/shard_map/psum | solution.py:157
  8.1 12.2 %collective-permute-start.1 = (f32[2,2,128]{2,1,0:T(2,128)S(1)}, f32[2,2,128]{2,1,0:T(2,128)S(1)}, u32[]{:S(2)}, u32[]{:S(2)}) collective-permute-start(f32[2,2,128]{2,1,0:T(2,128)S(1)} %pad_maximum_fusion.11), channel_id=1, source_target_pairs={{4,0},{8,4},{12,8},{0,12},{5,1},{9,5},{13,9},{1,13},{6,2},{10,6},{... | collective-permute-start | bytes 6152 | tf_op jit(solution)/shard_map/ppermute | solution.py:22
  12.3 8.1 %collective-permute-start = (f32[2,2,128]{2,1,0:T(2,128)S(1)}, f32[2,2,128]{2,1,0:T(2,128)S(1)}, u32[]{:S(2)}, u32[]{:S(2)}) collective-permute-start(f32[2,2,128]{2,1,0:T(2,128)S(1)} %pad_maximum_fusion.11), channel_id=1, source_target_pairs={{0,4},{4,8},{8,12},{12,0},{1,5},{5,9},{9,13},{13,1},{2,6},{6,10},{... | collective-permute-start | bytes 6152 | tf_op jit(solution)/shard_map/ppermute | solution.py:19
  14.4 28.2 %collective-permute-start.7 = (bf16[2,2,128,256]{3,2,0,1:T(8,128)(2,1)S(1)}, bf16[2,2,128,256]{3,2,0,1:T(8,128)(2,1)S(1)}, u32[]{:S(2)}, u32[]{:S(2)}) collective-permute-start(bf16[2,2,128,256]{3,2,0,1:T(8,128)(2,1)S(1)} %get-tuple-element.327), channel_id=1, source_target_pairs={{4,0},{8,4},{12,8},{0,12},{5,1},{9,5},{13,9},{1,13},{6,2},{10,6},{... | collective-permute-start | bytes 786440 | tf_op jit(solution)/shard_map/ppermute | solution.py:22
  17.7 26.6 %collective-permute-start.6 = (bf16[2,2,128,256]{3,2,0,1:T(8,128)(2,1)S(1)}, bf16[2,2,128,256]{3,2,0,1:T(8,128)(2,1)S(1)}, u32[]{:S(2)}, u32[]{:S(2)}) collective-permute-start(bf16[2,2,128,256]{3,2,0,1:T(8,128)(2,1)S(1)} %get-tuple-element.327), channel_id=1, source_target_pairs={{0,4},{4,8},{8,12},{12,0},{1,5},{5,9},{9,13},{13,1},{2,6},{6,10},{... | collective-permute-start | bytes 786440 | tf_op jit(solution)/shard_map/ppermute | solution.py:19
  18.6 4.9 copy-start.3
  18.6 4.9 copy-start.4
  18.7 4.9 copy-start.2
  23.7 4.2 collective-permute-start.3
  27.0 4.2 collective-permute-start.2
  34.6 2.5 collective-permute-start.5
  35.0 4.2 collective-permute-start.4
  57.1 7.5 %collective-permute-start.9 = (bf16[2,2,128,256]{3,2,0,1:T(8,128)(2,1)S(1)}, bf16[2,2,128,256]{3,2,0,1:T(8,128)(2,1)S(1)}, u32[]{:S(2)}, u32[]{:S(2)}) collective-permute-start(bf16[2,2,128,256]{3,2,0,1:T(8,128)(2,1)S(1)} %get-tuple-element.325), channel_id=1, source_target_pairs={{4,0},{8,4},{12,8},{0,12},{5,1},{9,5},{13,9},{1,13},{6,2},{10,6},{... | collective-permute-start | bytes 786440 | tf_op jit(solution)/shard_map/ppermute | solution.py:22
  58.0 8.5 %collective-permute-start.8 = (bf16[2,2,128,256]{3,2,0,1:T(8,128)(2,1)S(1)}, bf16[2,2,128,256]{3,2,0,1:T(8,128)(2,1)S(1)}, u32[]{:S(2)}, u32[]{:S(2)}) collective-permute-start(bf16[2,2,128,256]{3,2,0,1:T(8,128)(2,1)S(1)} %get-tuple-element.325), channel_id=1, source_target_pairs={{0,4},{4,8},{8,12},{12,0},{1,5},{5,9},{9,13},{13,1},{2,6},{6,10},{... | collective-permute-start | bytes 786440 | tf_op jit(solution)/shard_map/ppermute | solution.py:19
  79.4 5.5 collective-permute-start.11
  80.8 12.8 %collective-permute-start.10 = (bf16[2,2,128,256]{3,2,0,1:T(8,128)(2,1)S(1)}, bf16[2,2,128,256]{3,2,0,1:T(8,128)(2,1)S(1)}, u32[]{:S(2)}, u32[]{:S(2)}) collective-permute-start(bf16[2,2,128,256]{3,2,0,1:T(8,128)(2,1)S(1)} %get-tuple-element.322), channel_id=1, source_target_pairs={{0,4},{4,8},{8,12},{12,0},{1,5},{5,9},{9,13},{13,1},{2,6},{6,10},{... | collective-permute-start | bytes 786440 | tf_op jit(solution)/shard_map/ppermute | solution.py:19
  256.8 1.9 copy-start
  571.8 7.2 %copy-start.1 = (f32[8,128,128]{1,2,0:T(8,128)S(1)}, f32[8,128,128]{1,2,0:T(8,128)}, u32[]{:S(2)}) copy-start(f32[8,128,128]{1,2,0:T(8,128)} %custom-call.70) | copy-start | bytes 1572868
  595.5 24.2 %all-to-all-start.1 = ((f32[4,1,65536]{2,1,0:T(1,128)}), f32[4,1,65536]{2,1,0:T(1,128)S(1)}, u32[]{:S(2)}, u32[]{:S(2)}) async-start(f32[4,1,65536]{2,1,0:T(1,128)} %reshape.847), calls=%async_computation.1 | async-start | bytes 2097152 | tf_op jit(solution)/shard_map/all_to_all | solution.py:160
Sparse Core Ops, SparseCore 0:
  133.6 107.9 all-reduce.2
where the time goes:
time: 647 us; the launch traced here: 640 us
  other arithmetic  287 us (44%)
  waiting for transfers between devices  130 us (20%)
  matrix products  87.6 us (14%)
  local copies, waits for them, and re-layouts  71.5 us (11%)
  starting transfers between devices  21.9 us (3%)
  blocking collectives  21.8 us (3%)
  between operations  20.3 us (3%)
    another operation x31, other arithmetic, body(): factor = jnp.linalg.cholesky(gram * gram_scale)  173 us
    psum x1, waiting for transfers between devices, body(): gram = lax.psum(partial_value, ('space', 'tangent'))  108 us
    another operation x3, other arithmetic, body(): jax.scipy.linalg.solve_triangular(factor, flat_rows.T, lower=True)  86 us
    another operation x14, matrix products, body(): factor = jnp.linalg.cholesky(gram * gram_scale)  23.1 us
    another operation x24, local copies, waits for them, and re-layouts  23 us
    all_to_all x1, blocking collectives, body(): lax.all_to_all(final, 'tangent', split_axis=2, concat_axis=3, tiled=True)  21.8 us
    gather x1, local copies, waits for them, and re-layouts, body(): log_diag = jnp.log(jnp.diagonal(factor))  17.3 us
    another operation x15, matrix products, body(): jax.scipy.linalg.solve_triangular(factor, flat_rows.T, lower=True)  14.7 us
  transfers between devices with their start and end apart: 14, of which 9 were waited for; matrix products, arithmetic and copies ran while one was open for 6% of the time, Pallas kernels for 0%

commit v1 on v0

--- a/solution.py
+++ b/solution.py
@@ -157,8 +157,14 @@
     gram = lax.psum(partial_value, ("space", "tangent"))
     factor = jnp.linalg.cholesky(gram * gram_scale)
     solved = jax.scipy.linalg.solve_triangular(factor, flat_rows.T, lower=True).T
-    columns_out = lax.all_to_all(
-        solved.reshape(rows_form.shape), "tangent", split_axis=3, concat_axis=2, tiled=True
+    columns_out = jnp.concatenate(
+        lax.all_to_all(
+            jnp.stack(jnp.split(solved.reshape(rows_form.shape), lax.axis_size("tangent"), axis=3)),
+            "tangent",
+            0,
+            0,
+        ),
+        axis=2,
     )
     log_diag = jnp.log(jnp.diagonal(factor))
     stretch = lax.dynamic_slice_in_dim(log_diag, lax.axis_index("tangent") * block_cols, block_cols)

time: 647 us -> 627 us (0.969)
  local copies, waits for them, and re-layouts: 71.5 us -> 54.2 us
    unnamed x13 -> x11, local copies, waits for them, and re-layouts: 11.7 us -> 2.14 us
    another operation x24 -> x25, local copies, waits for them, and re-layouts: 23 us -> 23.2 us
where the time goes in v1:
time: 627 us; the launch traced here: 620 us
  other arithmetic  285 us (45%)
  waiting for transfers between devices  129 us (21%)
  matrix products  87.6 us (14%)
  local copies, waits for them, and re-layouts  54.2 us (9%)
  blocking collectives  21.8 us (3%)
  starting transfers between devices  21.6 us (3%)
  between operations  20.3 us (3%)
    another operation x31, other arithmetic, body(): factor = jnp.linalg.cholesky(gram * gram_scale)  173 us
    psum x1, waiting for transfers between devices, body(): gram = lax.psum(partial_value, ('space', 'tangent'))  108 us
    another operation x3, other arithmetic, body(): jax.scipy.linalg.solve_triangular(factor, flat_rows.T, lower=True)  86 us
    another operation x14, matrix products, body(): factor = jnp.linalg.cholesky(gram * gram_scale)  23.1 us
    another operation x24, local copies, waits for them, and re-layouts  23 us
    all_to_all x1, blocking collectives, body(): lax.all_to_all(final, 'tangent', split_axis=2, concat_axis=3, tiled=True)  21.8 us
    gather x1, local copies, waits for them, and re-layouts, body(): log_diag = jnp.log(jnp.diagonal(factor))  16.8 us
    another operation x15, matrix products, body(): jax.scipy.linalg.solve_triangular(factor, flat_rows.T, lower=True)  14.7 us
  transfers between devices with their start and end apart: 14, of which 9 were waited for; matrix products, arithmetic and copies ran while one was open for 6% of the time, Pallas kernels for 0%

profile of v1, /device:TPU:1, one launch (start us, length us, event | category | flops | bytes accessed | tf_op | source)
XLA Modules:
  0.0 619.7 jit_solution(3885132230414479871)
XLA Ops:
  8.1 4.2 collective-permute-start.1
  14.4 3.3 collective-permute-start.7
  20.4 3.1 convert_reduce_fusion.79
  23.7 3.3 collective-permute-start.3
  27.9 3.4 collective-permute-done.2
  31.3 3.1 convert_reduce_fusion.52
  39.3 3.6 convert_reduce_fusion.25
  59.9 4.8 collective-permute-done.9
  82.5 2.5 collective-permute-done.11
  86.7 7.0 %collective-permute-done.10 = bf16[2,2,128,256]{3,2,0,1:T(8,128)(2,1)S(1)} collective-permute-done((bf16[2,2,128,256]{3,2,0,1:T(8,128)(2,1)S(1)}, bf16[2,2,128,256]{3,2,0,1:T(8,128)(2,1)S(1)}, u32[]{:S(2)}, u32[]{:S(2)}) %collective-permute-start.10) | collective-permute-done | bytes 262176 | tf_op jit(solution)/shard_map/ppermute | solution.py:19
  105.7 21.8 %all_to_all.20 = f32[2,4,128,256]{3,0,1,2:T(2,128)S(1)} all-to-all(f32[2,4,128,256]{3,0,1,2:T(2,128)S(1)} %copy.24), channel_id=1, replica_groups=mesh['groups'=2,'space'=4,'tangent'=4] {'tangent'}, dimensions={2} | all-to-all | bytes 2097152 | tf_op jit(solution)/shard_map/all_to_all | solution.py:146
  128.4 5.2 fusion.2420
  133.9 107.7 %all-reduce.3.cloned.1.call-done = f32[1024,1024]{0,1:T(8,128)} async-done(((f32[1024,1024]{0,1:T(8,128)}), f32[1024,1024]{0,1:T(8,128)}) %all-reduce.3.cloned.1.call-update) | async-done | bytes 4194320 | tf_op jit(solution)/shard_map/psum | solution.py:157
  241.7 5.0 broadcast_multiply_fusion
  246.7 5.5 copy.27
  252.2 4.4 fusion
  258.6 11.7 %cholesky.187 = f32[128,128]{1,0:T(8,128)S(1)} custom-call(f32[128,128]{1,0:T(8,128)S(1)} %cholesky.514), custom_call_target="Cholesky" | custom-call | tf_op jit(solution)/shard_map/jit(cholesky)/cholesky | solution.py:158
  271.0 9.8 %custom-call.63 = f32[1,128,128]{1,2,0:T(8,128)S(1)} custom-call(f32[1,128,128]{2,1,0:T(8,128)S(1)} %get-tuple-element.436), custom_call_target="InvertDiagBlocksLowerTriangular" | custom-call | tf_op jit(solution)/shard_map/jit(cholesky)/cholesky | solution.py:158
  280.8 2.5 cholesky.218
  283.3 2.3 constant_dynamic-update-slice_fusion.32
  287.2 11.9 %cholesky.209 = f32[128,128]{1,0:T(8,128)S(1)} custom-call(f32[128,128]{1,0:T(8,128)S(1)} %cholesky.518), custom_call_target="Cholesky" | custom-call | tf_op jit(solution)/shard_map/jit(cholesky)/cholesky | solution.py:158
  300.4 9.8 %custom-call.64 = f32[1,128,128]{1,2,0:T(8,128)S(1)} custom-call(f32[1,128,128]{2,1,0:T(8,128)S(1)} %get-tuple-element.433), custom_call_target="InvertDiagBlocksLowerTriangular" | custom-call | tf_op jit(solution)/shard_map/jit(cholesky)/cholesky | solution.py:158
  313.5 11.7 %cholesky.402 = f32[128,128]{1,0:T(8,128)S(1)} custom-call(f32[128,128]{1,0:T(8,128)S(1)} %cholesky.523), custom_call_target="Cholesky" | custom-call | tf_op jit(solution)/shard_map/jit(cholesky)/cholesky | solution.py:158
  326.5 9.8 %custom-call.65 = f32[1,128,128]{1,2,0:T(8,128)S(1)} custom-call(f32[1,128,128]{2,1,0:T(8,128)S(1)} %get-tuple-element.430), custom_call_target="InvertDiagBlocksLowerTriangular" | custom-call | tf_op jit(solution)/shard_map/jit(cholesky)/cholesky | solution.py:158
  337.5 2.4 convolution_subtract_fusion.2
  339.9 12.1 %cholesky.421 = f32[128,128]{1,0:T(8,128)S(1)} custom-call(f32[128,128]{1,0:T(8,128)S(1)} %cholesky.528), custom_call_target="Cholesky" | custom-call | tf_op jit(solution)/shard_map/jit(cholesky)/cholesky | solution.py:158
  353.4 9.8 %custom-call.66 = f32[1,128,128]{1,2,0:T(8,128)S(1)} custom-call(f32[1,128,128]{2,1,0:T(8,128)S(1)} %get-tuple-element.427), custom_call_target="InvertDiagBlocksLowerTriangular" | custom-call | tf_op jit(solution)/shard_map/jit(cholesky)/cholesky | solution.py:158
  364.3 2.3 convolution_subtract_fusion.3
  366.6 11.7 %cholesky.440 = f32[128,128]{1,0:T(8,128)S(1)} custom-call(f32[128,128]{1,0:T(8,128)S(1)} %cholesky.533), custom_call_target="Cholesky" | custom-call | tf_op jit(solution)/shard_map/jit(cholesky)/cholesky | solution.py:158
  379.7 10.0 %custom-call.67 = f32[1,128,128]{1,2,0:T(8,128)S(1)} custom-call(f32[1,128,128]{2,1,0:T(8,128)S(1)} %get-tuple-element.424), custom_call_target="InvertDiagBlocksLowerTriangular" | custom-call | tf_op jit(solution)/shard_map/jit(cholesky)/cholesky | solution.py:158
  390.7 2.3 convolution_subtract_fusion.4
  393.0 11.7 %cholesky.460 = f32[128,128]{1,0:T(8,128)S(1)} custom-call(f32[128,128]{1,0:T(8,128)S(1)} %cholesky.538), custom_call_target="Cholesky" | custom-call | tf_op jit(solution)/shard_map/jit(cholesky)/cholesky | solution.py:158
  406.0 9.8 %custom-call.68 = f32[1,128,128]{1,2,0:T(8,128)S(1)} custom-call(f32[1,128,128]{2,1,0:T(8,128)S(1)} %get-tuple-element.421), custom_call_target="InvertDiagBlocksLowerTriangular" | custom-call | tf_op jit(solution)/shard_map/jit(cholesky)/cholesky | solution.py:158
  418.8 11.9 %cholesky.480 = f32[128,128]{1,0:T(8,128)S(1)} custom-call(f32[128,128]{1,0:T(8,128)S(1)} %cholesky.543), custom_call_target="Cholesky" | custom-call | tf_op jit(solution)/shard_map/jit(cholesky)/cholesky | solution.py:158
  432.0 9.8 %custom-call.69 = f32[1,128,128]{1,2,0:T(8,128)S(1)} custom-call(f32[1,128,128]{2,1,0:T(8,128)S(1)} %get-tuple-element.418), custom_call_target="InvertDiagBlocksLowerTriangular" | custom-call | tf_op jit(solution)/shard_map/jit(cholesky)/cholesky | solution.py:158
  444.4 11.7 %cholesky.498 = f32[128,128]{1,0:T(8,128)S(1)} custom-call(f32[128,128]{1,0:T(8,128)S(1)} %convolution_subtract_fusion.13), custom_call_target="Cholesky" | custom-call | tf_op jit(solution)/shard_map/jit(cholesky)/cholesky | solution.py:158
  462.5 6.6 %fusion.1 = (f32[1024,1024]{1,0:T(8,128)}, f32[1024,1024]{1,0:T(8,128)}) fusion(f32[1024,1024]{1,0:T(8,128)} %get-tuple-element.416, pred[]{:T(512)S(6)} %cholesky.513), kind=kLoop, calls=%fused_computation.7 | loop fusion | flops 4194304 | bytes 12582913 | tf_op jit(solution)/shard_map/jit(_solve_triangular)/triangular_solve | solution.py:159
  469.1 23.2 %while.1 = (s32[]{:T(128)}, f32[1024,1024]{1,0:T(8,128)}, s32[8,2]{0,1:T(2,128)S(1)}, f32[8,128,128]{2,1,0:T(8,128)S(1)}, s32[]{:T(128)}) while((s32[]{:T(128)}, f32[1024,1024]{1,0:T(8,128)}, s32[8,2]{0,1:T(2,128)S(1)}, f32[8,128,128]{2,1,0:T(8,128)S(1)}, s32[]{:T(128)}) %tuple.399), condition=%wide.while_cond, body=%wide.while_body.sunk | while | flops 2 | bytes 131189 | solution.py:159
  469.7 2.3 bitcast_dynamic-update-slice_fusion.2
  472.6 2.3 bitcast_dynamic-update-slice_fusion.2
  475.5 2.3 bitcast_dynamic-update-slice_fusion.2
  478.4 2.3 bitcast_dynamic-update-slice_fusion.2
  481.3 2.3 bitcast_dynamic-update-slice_fusion.2
  484.2 2.3 bitcast_dynamic-update-slice_fusion.2
  487.1 2.3 bitcast_dynamic-update-slice_fusion.2
  492.3 79.5 %custom-call.70 = f32[8,128,128]{1,2,0:T(8,128)} custom-call(f32[8,128,128]{2,1,0:T(8,128)S(1)} %get-tuple-element.10), custom_call_target="InvertDiagBlocksLowerTriangular" | custom-call | tf_op jit(solution)/shard_map/jit(_solve_triangular)/triangular_solve | solution.py:159
  588.1 5.3 all-to-all-start.1
  594.1 16.8 %gather_fusion = f32[1024]{0:T(1024)S(1)} fusion(f32[1024,1024]{1,0:T(8,128)} %get-tuple-element.320, s32[1024]{0:T(1024)S(1)} %bitcast.401), kind=kCustom, calls=%fused_computation | custom fusion | bytes 16384 | tf_op jit(solution)/shard_map/jit(diagonal)/cond/branch_0_fun/gather | solution.py:169
  (299 shorter events, 111.9 us)
Async XLA Ops:
  7.2 234.5 %all-reduce.3.cloned.1.call-start = ((), (), s32[]{:S(2)}) async-start(), calls=%async_computation.2 | async-start | bytes 8388608 | tf_op jit(solution)/shard_map/psum | solution.py:157
  8.1 12.2 %collective-permute-start.1 = (f32[2,2,128]{2,1,0:T(2,128)S(1)}, f32[2,2,128]{2,1,0:T(2,128)S(1)}, u32[]{:S(2)}, u32[]{:S(2)}) collective-permute-start(f32[2,2,128]{2,1,0:T(2,128)S(1)} %pad_maximum_fusion.12), channel_id=1, source_target_pairs={{4,0},{8,4},{12,8},{0,12},{5,1},{9,5},{13,9},{1,13},{6,2},{10,6},{... | collective-permute-start | bytes 6152 | tf_op jit(solution)/shard_map/ppermute | solution.py:22
  12.3 8.1 %collective-permute-start = (f32[2,2,128]{2,1,0:T(2,128)S(1)}, f32[2,2,128]{2,1,0:T(2,128)S(1)}, u32[]{:S(2)}, u32[]{:S(2)}) collective-permute-start(f32[2,2,128]{2,1,0:T(2,128)S(1)} %pad_maximum_fusion.12), channel_id=1, source_target_pairs={{0,4},{4,8},{8,12},{12,0},{1,5},{5,9},{9,13},{13,1},{2,6},{6,10},{... | collective-permute-start | bytes 6152 | tf_op jit(solution)/shard_map/ppermute | solution.py:19
  14.4 28.6 %collective-permute-start.7 = (bf16[2,2,128,256]{3,2,0,1:T(8,128)(2,1)S(1)}, bf16[2,2,128,256]{3,2,0,1:T(8,128)(2,1)S(1)}, u32[]{:S(2)}, u32[]{:S(2)}) collective-permute-start(bf16[2,2,128,256]{3,2,0,1:T(8,128)(2,1)S(1)} %get-tuple-element.327), channel_id=1, source_target_pairs={{4,0},{8,4},{12,8},{0,12},{5,1},{9,5},{13,9},{1,13},{6,2},{10,6},{... | collective-permute-start | bytes 786440 | tf_op jit(solution)/shard_map/ppermute | solution.py:22
  17.7 26.9 %collective-permute-start.6 = (bf16[2,2,128,256]{3,2,0,1:T(8,128)(2,1)S(1)}, bf16[2,2,128,256]{3,2,0,1:T(8,128)(2,1)S(1)}, u32[]{:S(2)}, u32[]{:S(2)}) collective-permute-start(bf16[2,2,128,256]{3,2,0,1:T(8,128)(2,1)S(1)} %get-tuple-element.327), channel_id=1, source_target_pairs={{0,4},{4,8},{8,12},{12,0},{1,5},{5,9},{9,13},{13,1},{2,6},{6,10},{... | collective-permute-start | bytes 786440 | tf_op jit(solution)/shard_map/ppermute | solution.py:19
  18.6 4.9 copy-start.3
  18.6 4.9 copy-start.4
  18.7 4.9 copy-start.2
  23.7 4.2 collective-permute-start.3
  27.0 4.2 collective-permute-start.2
  34.6 2.5 collective-permute-start.5
  35.0 4.2 collective-permute-start.4
  57.4 7.3 %collective-permute-start.9 = (bf16[2,2,128,256]{3,2,0,1:T(8,128)(2,1)S(1)}, bf16[2,2,128,256]{3,2,0,1:T(8,128)(2,1)S(1)}, u32[]{:S(2)}, u32[]{:S(2)}) collective-permute-start(bf16[2,2,128,256]{3,2,0,1:T(8,128)(2,1)S(1)} %get-tuple-element.325), channel_id=1, source_target_pairs={{4,0},{8,4},{12,8},{0,12},{5,1},{9,5},{13,9},{1,13},{6,2},{10,6},{... | collective-permute-start | bytes 786440 | tf_op jit(solution)/shard_map/ppermute | solution.py:22
  58.1 8.5 %collective-permute-start.8 = (bf16[2,2,128,256]{3,2,0,1:T(8,128)(2,1)S(1)}, bf16[2,2,128,256]{3,2,0,1:T(8,128)(2,1)S(1)}, u32[]{:S(2)}, u32[]{:S(2)}) collective-permute-start(bf16[2,2,128,256]{3,2,0,1:T(8,128)(2,1)S(1)} %get-tuple-element.325), channel_id=1, source_target_pairs={{0,4},{4,8},{8,12},{12,0},{1,5},{5,9},{9,13},{13,1},{2,6},{6,10},{... | collective-permute-start | bytes 786440 | tf_op jit(solution)/shard_map/ppermute | solution.py:19
  79.5 5.5 collective-permute-start.11
  80.9 12.8 %collective-permute-start.10 = (bf16[2,2,128,256]{3,2,0,1:T(8,128)(2,1)S(1)}, bf16[2,2,128,256]{3,2,0,1:T(8,128)(2,1)S(1)}, u32[]{:S(2)}, u32[]{:S(2)}) collective-permute-start(bf16[2,2,128,256]{3,2,0,1:T(8,128)(2,1)S(1)} %get-tuple-element.322), channel_id=1, source_target_pairs={{0,4},{4,8},{8,12},{12,0},{1,5},{5,9},{9,13},{13,1},{2,6},{6,10},{... | collective-permute-start | bytes 786440 | tf_op jit(solution)/shard_map/ppermute | solution.py:19
  256.6 1.9 copy-start
  571.7 7.2 %copy-start.1 = (f32[8,128,128]{1,2,0:T(8,128)S(1)}, f32[8,128,128]{1,2,0:T(8,128)}, u32[]{:S(2)}) copy-start(f32[8,128,128]{1,2,0:T(8,128)} %custom-call.70) | copy-start | bytes 1572868
  588.1 23.4 %all-to-all-start.1 = ((f32[4,2,4,32,256]{4,3,2,1,0:T(8,128)}), f32[4,2,4,32,256]{4,3,2,1,0:T(8,128)S(1)}, u32[]{:S(2)}, u32[]{:S(2)}) async-start(f32[4,2,4,32,256]{4,3,2,1,0:T(8,128)} %pad_maximum_fusion.1), calls=%async_computation.1 | async-start | bytes 2097152 | tf_op jit(solution)/shard_map/all_to_all | solution.py:161
Sparse Core Ops, SparseCore 0:
  133.7 107.9 all-reduce.2
